TPU v7x, 32 devices: a whole 2x2x4 slice. The times are simulated.
32 devices in a mesh: dp: 8 (over z, core), tensor: 4 (over y, x).
Axes of the slice: x: 2, y: 2, z: 4, core: 2. Of those that a mesh axis runs over, the one named last changes fastest.
Arguments:
- hidden_input: bfloat16 [8192, 8192], P('dp', 'tensor'), may hold values from -6 to 6
- key_value_weight: bfloat16 [8192, 2048], P('tensor'), may hold values from -0.0625 to 0.0625
- adapter_down_weight: bfloat16 [128, 8192, 128], P('dp', 'tensor'), may hold values from -0.0625 to 0.0625
- adapter_up_weight: bfloat16 [128, 64, 2048], P('dp', None, 'tensor'), may hold values from -0.75 to 0.75
- queries: bfloat16 [8, 8192, 8, 128], P('tensor', 'dp'), may hold values from -12 to 12
- key_value_cache: bfloat16 [2, 8, 8192, 32, 128], P(None, 'tensor', 'dp'), may hold values from -12 to 12
- request_adapter_index: int32 [8192], P('dp'), may hold values from 0 to 127, as said below
- cached_length: int32 [8192], P('dp'), may hold values from 2 to 32
Outputs:
- new_kv: bfloat16 [2, 8, 8192, 128], P(None, 'tensor', 'dp')
- attn_out: bfloat16 [8, 8192, 8, 128], P('tensor', 'dp')
Inputs may be any that keep to these rules, and one draw needn't show every extreme that they name: Write owner(r) = request_adapter_index[r] // 16. In each block of 1024 requests (those of one index of dp) owner(r) never falls from one request to the next; at most 256 requests of a block name one owner, and one owner is named by exactly 256 requests of every block.
All inputs are finite; a program needn't handle non-finite values.
Results may differ from a plain program's by a relative error of at most 0.009.
Values may be sent and summed in bfloat16 or wider, within the bound.
A program may use at most 192 MiB of HBM per device.

v0:
```python
import jax
import jax.numpy as jnp
from jax import lax
from jax.sharding import PartitionSpec as P

rope_theta = 500000.0


def rotate_keys(key_rows, positions):
    head_size = key_rows.shape[-1]
    half_dim = head_size // 2
    freq_index = jnp.arange(half_dim).astype(key_rows.dtype)
    inverse = rope_theta ** (-(2.0 * freq_index / head_size))
    angles = positions[..., None].astype(key_rows.dtype) * inverse
    cosine = jnp.cos(angles)
    sine_part = jnp.sin(angles)
    first_half = key_rows[..., :half_dim]
    second_half = key_rows[..., half_dim:]
    return jnp.concatenate(
        [
            first_half * cosine - second_half * sine_part,
            second_half * cosine + first_half * sine_part,
        ],
        axis=-1,
    )


def attend(query_rows, cache_keys, cache_values, new_keys, new_values, lengths):
    score_scale = 1.0 / jnp.sqrt(jnp.float32(query_rows.shape[-1]))
    cache_scores = (
        jnp.einsum("igd,icd->igc", query_rows, cache_keys, preferred_element_type=jnp.float32)
        * score_scale
    )
    own_scores = (
        jnp.einsum("igd,id->ig", query_rows, new_keys, preferred_element_type=jnp.float32)
        * score_scale
    )
    valid_mask = (jnp.arange(cache_keys.shape[1])[None, :] < lengths[:, None])[:, None, :]
    masked = jnp.where(valid_mask, cache_scores, -1e30)
    peak_score = jnp.maximum(jnp.max(masked, axis=-1), own_scores)
    cache_exp = jnp.where(valid_mask, jnp.exp(masked - peak_score[..., None]), 0.0)
    own_exp = jnp.exp(own_scores - peak_score)
    denominator = jnp.sum(cache_exp, axis=-1) + own_exp
    cache_weights = (cache_exp / denominator[..., None]).astype(jnp.bfloat16)
    own_weights = (own_exp / denominator).astype(jnp.bfloat16)
    attended = jnp.einsum(
        "igc,icd->igd", cache_weights, cache_values, preferred_element_type=jnp.float32
    )
    attended = (
        attended
        + own_weights.astype(jnp.float32)[..., None] * new_values.astype(jnp.float32)[:, None, :]
    )
    return attended.astype(jnp.bfloat16)


def per_device(
    hidden_input,
    key_value_weight,
    adapter_down_weight,
    adapter_up_weight,
    queries,
    key_value_cache,
    request_adapter_index,
    cached_length,
):
    row_count, feat_count = hidden_input.shape
    owner_count = lax.axis_size("dp")
    adapter_total = adapter_down_weight.shape[0]
    adapter_rank_width = adapter_down_weight.shape[2] // 2
    column_extent = adapter_up_weight.shape[2]
    head_dim = queries.shape[3]
    heads_here = queries.shape[0]
    rows_here = queries.shape[1]
    split_count = row_count // rows_here
    capacity = 2 * row_count // owner_count
    kv_heads = key_value_weight.shape[1] // (2 * head_dim)
    tensor_index = lax.axis_index("tensor")
    owner_of = request_adapter_index // adapter_total
    owner_match = (owner_of[:, None] == jnp.arange(owner_count)[None, :]).astype(jnp.int32)
    counts = jnp.sum(owner_match, axis=0)
    starts = jnp.cumsum(counts) - counts
    slot_rows = starts[:, None] + jnp.arange(capacity)[None, :]
    padded_rows = jnp.concatenate(
        [hidden_input, jnp.zeros((capacity, feat_count), hidden_input.dtype)], axis=0
    )
    local_ids = request_adapter_index - owner_of * adapter_total
    padded_ids = jnp.concatenate([local_ids, jnp.zeros((capacity,), jnp.int32)])
    slot_live = jnp.arange(capacity)[None, :] < counts[:, None]
    send_rows = jnp.take(padded_rows, slot_rows, axis=0)
    send_ids = jnp.where(slot_live, jnp.take(padded_ids, slot_rows, axis=0), -1).astype(
        jnp.bfloat16
    )
    column_piece = (tensor_index * column_extent + jnp.arange(column_extent)) // head_dim
    key_columns = column_piece % 2 == 0
    raised_flattened = adapter_up_weight.reshape(adapter_total * adapter_rank_width, column_extent)
    rows_in = lax.all_to_all(send_rows, "dp", split_axis=0, concat_axis=0, tiled=True)
    ids_in = lax.all_to_all(send_ids, "dp", split_axis=0, concat_axis=0, tiled=True)
    sources, item_count = ids_in.shape
    flattened_rows = rows_in.reshape(sources * item_count, feat_count)
    flat_ids = ids_in.reshape(sources * item_count)
    one_hot = (flat_ids[:, None] == jnp.arange(adapter_total).astype(jnp.bfloat16)[None, :]).astype(
        jnp.bfloat16
    )
    matrix_products = jnp.einsum(
        "nt,wtz->nwz", flattened_rows, adapter_down_weight, preferred_element_type=jnp.float32
    )
    partial_rank = jnp.sum(matrix_products * one_hot[:, :, None], axis=1)
    full_rank = lax.psum(partial_rank, "tensor").astype(jnp.bfloat16)
    chosen = one_hot[:, :, None] * full_rank[:, None, :]
    key_rank = chosen[:, :, :adapter_rank_width].reshape(
        sources * item_count, adapter_total * adapter_rank_width
    )
    value_rank = chosen[:, :, adapter_rank_width:].reshape(
        sources * item_count, adapter_total * adapter_rank_width
    )
    key_delta = jnp.dot(key_rank, raised_flattened, preferred_element_type=jnp.float32)
    value_delta = jnp.dot(value_rank, raised_flattened, preferred_element_type=jnp.float32)
    delta_cols = jnp.where(key_columns[None, :], key_delta, value_delta).astype(jnp.bfloat16)
    delta_cols = delta_cols.reshape(sources, item_count, column_extent)
    returned = lax.all_to_all(delta_cols, "dp", split_axis=0, concat_axis=0, tiled=True)
    slot_index = owner_of * capacity + (jnp.arange(row_count) - jnp.take(starts, owner_of))
    delta_rows = jnp.take(
        returned.reshape(owner_count * capacity, column_extent), slot_index, axis=0
    )
    base_sum = jnp.dot(hidden_input, key_value_weight, preferred_element_type=jnp.float32)
    column_start = tensor_index * column_extent
    own_columns = lax.dynamic_slice_in_dim(
        base_sum, column_start, column_extent, 1
    ) + delta_rows.astype(jnp.float32)
    partial_value = lax.dynamic_update_slice_in_dim(base_sum, own_columns, column_start, 1)
    first_row = tensor_index * heads_here
    half_index = first_row % split_count
    head_start = first_row // split_count
    head_span = (heads_here + split_count - 1) // split_count
    summed = lax.psum(partial_value, "tensor")
    summed_view = summed.reshape(split_count, rows_here, kv_heads, 2, head_dim)
    own_part = lax.dynamic_slice(
        summed_view, (half_index, 0, head_start, 0, 0), (1, rows_here, head_span, 2, head_dim)
    )[0]
    fresh_kv = jnp.transpose(own_part, (2, 1, 0, 3))
    lens_here = lax.dynamic_slice_in_dim(cached_length, half_index * rows_here, rows_here, 0)
    new_keys = rotate_keys(fresh_kv[0], lens_here[None, :])
    new_kv = jnp.stack([new_keys, fresh_kv[1]]).astype(jnp.bfloat16)
    flat_count = heads_here * rows_here
    cache_slots = key_value_cache.shape[3]
    attn_out = attend(
        queries.reshape(flat_count, queries.shape[2], head_dim),
        key_value_cache[0].reshape(flat_count, cache_slots, head_dim),
        key_value_cache[1].reshape(flat_count, cache_slots, head_dim),
        new_kv[0].reshape(flat_count, head_dim),
        new_kv[1].reshape(flat_count, head_dim),
        jnp.tile(lens_here, heads_here),
    ).reshape(queries.shape)
    return (new_kv, attn_out)


def solution(mesh):
    return jax.shard_map(
        per_device,
        mesh=mesh,
        in_specs=(
            P("dp", "tensor"),
            P("tensor", None),
            P("dp", "tensor", None),
            P("dp", None, "tensor"),
            P("tensor", "dp", None, None),
            P(None, "tensor", "dp", None, None),
            P("dp"),
            P("dp"),
        ),
        out_specs=(P(None, "tensor", "dp", None), P("tensor", "dp", None, None)),
        check_vma=False,
    )
```

profile of v0, /device:TPU:1, one launch (start us, length us, event | category | flops | bytes accessed | tf_op | source)
XLA Modules:
  0.0 635.7 jit_solution(4527441967412829695)
XLA Ops:
  7.2 0.0 copy-start
  7.2 0.8 add_select_fusion
  8.0 0.1 convert_reduce_fusion
  8.1 0.2 reduce-window.7
  8.3 0.1 fusion.21
  8.4 11.8 %gather_fusion = s32[2048]{0:T(1024)S(1)} fusion(s32[1280]{0:T(1024)S(1)} %concatenate.10, s32[2048]{0:T(1024)S(1)} %broadcast_clamp_fusion), kind=kCustom, calls=%fused_computation | custom fusion | bytes 24576 | tf_op jit(solution)/shard_map/jit(_take)/gather | solution.py:90
  20.2 0.1 fusion.22
  20.3 0.5 broadcast.387
  20.8 0.7 reduce.1
  21.5 0.6 reshape.456
  22.1 6.4 %all-to-all-start = ((bf16[8,2,128]{2,1,0:T(2,128)(2,1)}), bf16[8,2,128]{2,1,0:T(2,128)(2,1)S(1)}, u32[]{:S(2)}, u32[]{:S(2)}) async-start(bf16[8,2,128]{2,1,0:T(2,128)(2,1)} %reshape.456), calls=%async_computation | async-start | bytes 8192 | tf_op jit(solution)/shard_map/all_to_all | solution.py:97
  28.4 0.1 fusion.25
  28.5 5.3 concatenate.11
  33.8 19.5 %gather_fusion.1 = bf16[2048,2048]{1,0:T(8,128)(2,1)} fusion(bf16[1280,2048]{1,0:T(8,128)(2,1)} %concatenate.11, s32[2048]{0:T(1024)S(1)} %broadcast_clamp_fusion), kind=kCustom, calls=%fused_computation.1 | custom fusion | bytes 16785408 | tf_op jit(solution)/shard_map/jit(_take)/gather | solution.py:89
  53.3 7.4 %broadcast_select_fusion = bf16[8,256,2048]{2,1,0:T(8,128)(2,1)} fusion(bf16[8,256,2048]{2,1,0:T(8,128)(2,1)} %bitcast.82, pred[8,256]{1,0:T(8,128)(4,1)S(1)} %fusion.25), kind=kLoop, calls=%fused_computation.8 | loop fusion | flops 4194304 | bytes 16779264 | tf_op jit(solution)/shard_map/jit(_take)/select_n | solution.py:89
  60.7 0.0 all-to-all-done
  60.7 5.1 all-to-all-start.1
  65.9 0.1 compare_convert_fusion
  66.0 183.0 %all-to-all-done.1 = bf16[8,256,2048]{2,1,0:T(8,128)(2,1)} async-done(((bf16[8,256,2048]{2,1,0:T(8,128)(2,1)}), bf16[8,256,2048]{2,1,0:T(8,128)(2,1)}, u32[]{:S(2)}, u32[]{:S(2)}) %all-to-all-start.1) | async-done | bytes 8388640 | tf_op jit(solution)/shard_map/all_to_all | solution.py:96
  249.0 22.3 %multiply_reduce_fusion = f32[2048,128]{1,0:T(8,128)S(1)} fusion(f32[2048,16]{0,1:T(8,128)S(1)} %get-tuple-element.13, bf16[2048,2048,1]{1,0,2:T(8,128)(2,1)} %bitcast.13, bf16[16,2048,128]{2,1,0:T(8,128)(2,1)} %param.10), kind=kOutput, calls=%fused_computation.3 | convolution fusion | flops 17187995648 | bytes 17956864 | tf_op jit(solution)/shard_map/nt,wtz->nwz/dot_general | solution.py:104
  271.2 39.2 %all-reduce.6 = bf16[2048,128]{1,0:T(8,128)(2,1)S(1)} all-reduce(f32[2048,128]{1,0:T(8,128)S(1)} %multiply_reduce_fusion), channel_id=1, replica_groups=mesh['dp'=8,'tensor'=4] {'tensor'}, use_global_device_ids=true, to_apply=%region_3.4 | all-reduce | flops 262144 | bytes 1572864 | tf_op jit(solution)/shard_map/psum | solution.py:108
  310.4 0.2 copy.21
  310.6 0.7 broadcast_multiply_fusion
  311.4 0.0 copy-done
  311.4 2.5 fusion.3
  313.8 0.0 copy-start.3
  313.8 3.8 fusion.7
  317.7 6.4 %all-to-all-start.2 = ((bf16[8,256,512]{2,1,0:T(8,128)(2,1)}), bf16[8,256,512]{2,1,0:T(8,128)(2,1)S(1)}, u32[]{:S(2)}, u32[]{:S(2)}) async-start(bf16[8,256,512]{2,1,0:T(8,128)(2,1)} %bitcast.88), calls=%async_computation.2 | async-start | bytes 4194304 | tf_op jit(solution)/shard_map/all_to_all | solution.py:120
  324.1 0.2 all-reduce.5.cloned.1.call-start
  324.3 0.7 fusion.43
  324.9 5.0 compare_and_fusion
  329.9 14.4 %fusion.44 = f32[1024,2048]{1,0:T(8,128)} fusion(bf16[1024,2048]{1,0:T(8,128)(2,1)} %param.8, bf16[2048,2048]{1,0:T(8,128)(2,1)} %param.9), kind=kOutput, calls=%fused_computation.103 | convolution fusion | flops 8589934592 | bytes 20971520 | tf_op jit(solution)/shard_map/dot_general | solution.py:125
  344.4 28.0 %all-to-all-done.2 = bf16[8,256,512]{2,1,0:T(8,128)(2,1)S(1)} async-done(((bf16[8,256,512]{2,1,0:T(8,128)(2,1)}), bf16[8,256,512]{2,1,0:T(8,128)(2,1)S(1)}, u32[]{:S(2)}, u32[]{:S(2)}) %all-to-all-start.2) | async-done | bytes 2097184 | tf_op jit(solution)/shard_map/all_to_all | solution.py:120
  372.3 4.0 gather_fusion.2
  376.3 3.3 add_dynamic-update-slice_fusion
  379.6 11.7 %reshape.402 = f32[1,1024,8,2,128]{4,3,2,1,0:T(2,128)} reshape(f32[1024,2048]{1,0:T(8,128)} %add_dynamic-update-slice_fusion) | data formatting | bytes 16777216 | tf_op jit(solution)/shard_map/reshape | solution.py:136
  391.3 0.0 all-reduce.5.cloned.1.call-update
  391.3 0.7 copy-done.4
  392.0 0.3 iota_compare_fusion
  392.3 24.5 %fusion.42 = (bf16[1,2,1024,32,128]{4,3,2,1,0:T(8,128)(2,1)}, bf16[1,2,1024,32,128]{4,3,2,1,0:T(8,128)(2,1)}) fusion(bf16[2,2,1024,32,128]{4,3,2,1,0:T(8,128)(2,1)} %param.13), kind=kLoop, calls=%fused_computation.101 | loop fusion | bytes 67108864 | tf_op jit(solution)/shard_map/slice | solution.py:149
  416.8 15.6 %fusion = (f32[2048,8]{1,0:T(8,128)S(1)}, f32[2048,8,32]{2,1,0:T(8,128)}) fusion(pred[2048,32]{1,0:T(8,128)(4,1)S(1)} %iota_compare_fusion, bf16[2048,8,128]{2,1,0:T(8,128)(2,1)} %bitcast.86, bf16[2048,32,128]{2,1,0:T(8,128)(2,1)} %bitcast.80), kind=kOutput, calls=%fused_computation.9 | convolution fusion | flops 135774208 | bytes 23199744 | tf_op jit(solution)/shard_map/igd,icd->igc/dot_general | solution.py:31
  432.4 0.3 copy.23
  432.7 1.9 multiply_cosine_fusion
  434.6 127.6 %all-reduce.5.cloned.1.call-done = f32[1,1024,8,2,128]{4,3,2,1,0:T(2,128)} async-done(((f32[1,1024,8,2,128]{4,3,2,1,0:T(2,128)}), f32[1,1024,8,2,128]{4,3,2,1,0:T(2,128)}) %all-reduce.5.cloned.1.call-update) | async-done | bytes 8388624 | tf_op jit(solution)/shard_map/psum | solution.py:135
  562.2 2.3 constant_dynamic-slice_fusion
  564.5 0.0 copy-start.2
  564.5 0.1 copy.37
  564.7 0.1 slice.68
  564.8 0.1 slice_bitcast_fusion
  564.8 0.4 subtract_convert_fusion
  565.3 0.3 fusion.55
  565.6 0.3 pad_maximum_fusion.1
  565.9 0.9 copy-done.2
  566.7 2.3 fusion.16
  569.0 0.5 copy.29
  569.5 0.1 bitcast_convert_fusion
  569.6 1.1 pad_maximum_fusion
  570.7 0.3 copy.24
  571.0 30.1 %fusion.1 = f32[2048,8]{1,0:T(8,128)S(1)} fusion(f32[2048,8,32]{2,1,0:T(8,128)} %get-tuple-element.25, f32[2048,8]{1,0:T(8,128)S(1)} %copy.24, pred[2048,32]{1,0:T(8,128)(4,1)S(1)} %iota_compare_fusion), kind=kLoop, calls=%fused_computation.10 | loop fusion | flops 2605056 | bytes 2293760 | tf_op jit(solution)/shard_map/reduce_sum | solution.py:43
  601.2 0.9 copy.25
  602.1 0.9 fusion.20
  603.0 1.4 copy.26
  604.4 1.3 copy.27
  605.7 22.9 %add_convert_fusion = bf16[2048,8,128]{2,1,0:T(8,128)(2,1)} fusion(f32[2048,128]{1,0:T(8,128)S(1)} %bitcast_convert_fusion, f32[2048,8]{1,0:T(8,128)} %copy.27, bf16[2048,32,128]{2,1,0:T(8,128)(2,1)} %bitcast.83, f32[2048,8,32]{2,1,0:T(8,128)} %get-tuple-element.25, f32[2048,8]{1,0:T(8,128)} %copy.26, f32[2048,8]{1,0:T(8,128)S(1)} %copy.24, ...), kind=kOutput, calls=%fused_computation.4 | convolution fusion | flops 143654912 | bytes 24379392 | tf_op jit(solution)/shard_map/igc,icd->igd/dot_general | solution.py:46
  (19 shorter events, 0.1 us)
Async XLA Ops:
  7.2 304.2 %copy-start = (bf16[16,64,512]{2,1,0:T(8,128)(2,1)S(1)}, bf16[16,64,512]{2,1,0:T(8,128)(2,1)}, u32[]{:S(2)}) copy-start(bf16[16,64,512]{2,1,0:T(8,128)(2,1)} %param.11) | copy-start | bytes 3145732
  22.1 38.7 %all-to-all-start = ((bf16[8,2,128]{2,1,0:T(2,128)(2,1)}), bf16[8,2,128]{2,1,0:T(2,128)(2,1)S(1)}, u32[]{:S(2)}, u32[]{:S(2)}) async-start(bf16[8,2,128]{2,1,0:T(2,128)(2,1)} %reshape.456), calls=%async_computation | async-start | bytes 8192 | tf_op jit(solution)/shard_map/all_to_all | solution.py:97
  60.7 188.2 %all-to-all-start.1 = ((bf16[8,256,2048]{2,1,0:T(8,128)(2,1)}), bf16[8,256,2048]{2,1,0:T(8,128)(2,1)}, u32[]{:S(2)}, u32[]{:S(2)}) async-start(bf16[8,256,2048]{2,1,0:T(8,128)(2,1)} %broadcast_select_fusion), calls=%async_computation.1 | async-start | bytes 16777216 | tf_op jit(solution)/shard_map/all_to_all | solution.py:96
  313.8 11.1 %copy-start.3 = (s32[1024]{0:T(1024)S(1)}, s32[1024]{0:T(1024)}, u32[]{:S(2)}) copy-start(s32[1024]{0:T(1024)} %param.14) | copy-start | bytes 12292
  317.7 54.6 %all-to-all-start.2 = ((bf16[8,256,512]{2,1,0:T(8,128)(2,1)}), bf16[8,256,512]{2,1,0:T(8,128)(2,1)S(1)}, u32[]{:S(2)}, u32[]{:S(2)}) async-start(bf16[8,256,512]{2,1,0:T(8,128)(2,1)} %bitcast.88), calls=%async_computation.2 | async-start | bytes 4194304 | tf_op jit(solution)/shard_map/all_to_all | solution.py:120
  324.1 238.1 %all-reduce.5.cloned.1.call-start = ((), (), s32[]{:S(2)}) async-start(), calls=%async_computation.3 | async-start | bytes 16777216 | tf_op jit(solution)/shard_map/psum | solution.py:135
  391.3 0.7 copy-start.4
  564.5 2.2 copy-start.2
  605.7 22.9 %copy-start.1 = (bf16[16,64,512]{2,1,0:T(8,128)(2,1)S(1)}, bf16[16,64,512]{2,1,0:T(8,128)(2,1)}, u32[]{:S(2)}) copy-start(bf16[16,64,512]{2,1,0:T(8,128)(2,1)} %param.11) | copy-start | bytes 3145732
Sparse Core Ops, SparseCore 0:
  391.4 170.7 all-reduce.4
where the time goes:
time: 643 us; the launch traced here: 636 us
  waiting for transfers between devices  339 us (53%)
  local copies, waits for them, and re-layouts  87.7 us (14%)
  matrix products  83.8 us (13%)
  other arithmetic  54 us (8%)
  blocking collectives  39.2 us (6%)
  starting transfers between devices  18.1 us (3%)
  between operations  14.5 us (2%)
    all_to_all x1, waiting for transfers between devices, per_device(): lax.all_to_all(send_rows, 'dp', split_axis=0, concat_axis=0, tiled=True)  183 us
    psum x1, waiting for transfers between devices, per_device(): summed = lax.psum(partial_value, 'tensor')  128 us
    psum x1, blocking collectives, per_device(): full_rank = lax.psum(partial_rank, 'tensor').astype(jnp.bfloat16)  39.2 us
    reduce_sum x1, other arithmetic, attend(): denominator = jnp.sum(cache_exp, axis=-1) + own_exp  30.1 us
    all_to_all x1, waiting for transfers between devices, per_device(): lax.all_to_all(delta_cols, 'dp', split_axis=0, concat_axis=0, tiled=True)  28 us
    slice x1, local copies, waits for them, and re-layouts, per_device(): key_value_cache[1].reshape(flat_count, cache_slots, head_dim)  24.5 us
    dot_general x1, matrix products, attend(): jnp.einsum('igc,icd->igd', cache_weights, cache_values, preferred_element...  22.9 us
    dot_general x1, matrix products, per_device(): jnp.einsum('nt,wtz->nwz', flattened_rows, adapter_down_weight, preferred_...  22.3 us
  transfers between devices with their start and end apart: 4, of which 3 were waited for; matrix products, arithmetic and copies ran while one was open for 15% of the time, Pallas kernels for 0%

commit v1 on v0

--- a/solution.py
+++ b/solution.py
@@ -1,9 +1,390 @@
+import functools
+
 import jax
 import jax.numpy as jnp
 from jax import lax
+from jax.experimental import pallas as pl
+from jax.experimental.pallas import tpu as pltpu
 from jax.sharding import PartitionSpec as P
 
 rope_theta = 500000.0
+MESH = pl.DeviceIdType.MESH
+BF = jnp.bfloat16
+F32 = jnp.float32
+CHUNKS = 4
+BIG = -1e30
+
+
+def project_kernel(
+    n, m, adapters, hid, idr, idc, w_hbm, dn_hbm, up_hbm, fresh,
+    wv, dv, uv, stage, recv, idsend, idrecv, idb, part, rsrecv, rkown, rkrecv, dout, ret,
+    load_sem, row_s, row_r, id_s, id_r, rs_s, rs_r, rk_s, rk_r, dl_s, dl_r,
+):
+    me = lax.axis_index("dp")
+    mt = lax.axis_index("tensor")
+    rows, feats = hid.shape
+    cap = stage.shape[1]
+    step = cap // CHUNKS
+    cols = fresh.shape[1]
+    far = sorted(range(1, n), key=lambda k: (abs(k - n // 2), k))
+
+    def dp_of(k):
+        return lax.rem(me + k + n, n)
+
+    def tp_of(k):
+        return lax.rem(mt + k + m, m)
+
+    barrier = pltpu.get_barrier_semaphore()
+    for k in range(1, n):
+        pl.semaphore_signal(barrier, inc=1, device_id=(dp_of(k), mt), device_id_type=MESH)
+    for k in range(1, m):
+        pl.semaphore_signal(barrier, inc=1, device_id=(me, tp_of(k)), device_id_type=MESH)
+    loads = [
+        pltpu.make_async_copy(w_hbm, wv, load_sem.at[0]),
+        pltpu.make_async_copy(dn_hbm, dv, load_sem.at[1]),
+        pltpu.make_async_copy(up_hbm, uv, load_sem.at[2]),
+    ]
+    for load in loads:
+        load.start()
+    pl.semaphore_wait(barrier, n - 1 + m - 1)
+
+    def row_copy(c, k):
+        return pltpu.make_async_remote_copy(
+            src_ref=stage.at[k, pl.ds(pl.multiple_of(c * step, step), step)],
+            dst_ref=recv.at[c, k],
+            send_sem=row_s.at[c, k], recv_sem=row_r.at[c, k],
+            device_id=(dp_of(k), mt), device_id_type=MESH,
+        )
+
+    def id_copy(k):
+        return pltpu.make_async_remote_copy(
+            src_ref=idsend.at[k], dst_ref=idrecv.at[k],
+            send_sem=id_s.at[k], recv_sem=id_r.at[k],
+            device_id=(dp_of(k), mt), device_id_type=MESH,
+        )
+
+    def rs_copy(k):
+        return pltpu.make_async_remote_copy(
+            src_ref=part.at[k], dst_ref=rsrecv.at[k],
+            send_sem=rs_s.at[k], recv_sem=rs_r.at[k],
+            device_id=(me, tp_of(k)), device_id_type=MESH,
+        )
+
+    def rank_copy(c, k):
+        return pltpu.make_async_remote_copy(
+            src_ref=rkown.at[c], dst_ref=rkrecv.at[c, k],
+            send_sem=rk_s.at[c, k], recv_sem=rk_r.at[c, k],
+            device_id=(me, tp_of(k)), device_id_type=MESH,
+        )
+
+    def delta_copy(c, k):
+        return pltpu.make_async_remote_copy(
+            src_ref=dout.at[c, k], dst_ref=ret.at[c, k],
+            send_sem=dl_s.at[c, k], recv_sem=dl_r.at[c, k],
+            device_id=(dp_of(-k), mt), device_id_type=MESH,
+        )
+
+    ids_row = idr[0:1, :]
+
+    def start_of(owner):
+        below = jnp.where(ids_row < owner * adapters, 1.0, 0.0)
+        return jnp.minimum(jnp.sum(below, axis=1, keepdims=True), float(rows - cap))
+
+    gap = (
+        lax.broadcasted_iota(jnp.int32, (cap, rows), 1)
+        - lax.broadcasted_iota(jnp.int32, (cap, rows), 0)
+    ).astype(F32)
+    width = 512
+    for k in far + [0]:
+        owner = dp_of(k)
+        pick = jnp.where(gap == start_of(owner), 1.0, 0.0).astype(BF)
+        local = (ids_row - owner * adapters).astype(F32)
+        local = jnp.broadcast_to(local, (16, rows)).astype(BF)
+        picked = lax.dot_general(
+            local, pick, (((1,), (1,)), ((), ())), preferred_element_type=F32
+        ).astype(BF)
+        if k == 0:
+            idrecv[0] = picked
+        else:
+            idsend[k] = picked
+            id_copy(k).start()
+
+        def fill(j, carry):
+            at = pl.ds(pl.multiple_of(j * width, width), width)
+            block = jnp.dot(pick, hid[:, at], preferred_element_type=F32).astype(BF)
+            if k == 0:
+                for c in range(CHUNKS):
+                    recv[c, 0, :, at] = block[c * step:(c + 1) * step]
+            else:
+                stage[k, :, at] = block
+            return carry
+
+        lax.fori_loop(0, feats // width, fill, 0)
+        if k:
+            row_copy(0, k).start()
+            row_copy(1, k).start()
+
+    loads[0].wait()
+    tile = 256
+    for k in list(range(1, m)) + [0]:
+        at = pl.ds(pl.multiple_of(tp_of(k) * cols, cols), cols)
+
+        def base(i, carry):
+            rs = pl.ds(pl.multiple_of(i * tile, tile), tile)
+            got = jnp.dot(hid[rs, :], wv[:, at], preferred_element_type=F32)
+            if k == 0:
+                fresh[rs, :] = got
+            else:
+                part[k, rs, :] = got.astype(BF)
+            return carry
+
+        lax.fori_loop(0, rows // tile, base, 0)
+        if k:
+            rs_copy(k).start()
+
+    eye = lax.broadcasted_iota(jnp.int32, (cap, cap), 0) == lax.broadcasted_iota(
+        jnp.int32, (cap, cap), 1
+    )
+    for k in range(n):
+        if k:
+            id_copy(k).wait()
+        line = idrecv[k, 0:1, :].astype(F32)
+        col = jnp.sum(jnp.where(eye, line, 0.0), axis=1, keepdims=True)
+        col = jnp.broadcast_to(col, (cap, 128))
+        for c in range(CHUNKS):
+            idb[c, k * step:(k + 1) * step, :] = col[c * step:(c + 1) * step]
+
+    for k in range(1, m):
+        rs_copy(k).wait()
+    loads[1].wait()
+    loads[2].wait()
+
+    lane = lax.broadcasted_iota(jnp.int32, (n * step, 128), 1)
+    upper = jnp.where(lane < 64, 0.0, 1.0)
+    halves = 2
+    group = n // halves
+
+    def chunk(c, carry):
+        for k in range(1, n):
+            row_copy(c, k).wait_send()
+
+        @pl.when(c < CHUNKS - 2)
+        def _():
+            for k in far:
+                row_copy(c + 2, k).start()
+
+        for k in range(1, n):
+            row_copy(c, k).wait_recv()
+        for h in range(halves):
+            block = recv[c, h * group:(h + 1) * group].reshape(group * step, feats)
+            which = idb[c, h * group * step:(h + 1) * group * step, :]
+
+            def pair(j, acc):
+                both = jnp.concatenate([dv[2 * j], dv[2 * j + 1]], axis=1)
+                got = jnp.dot(block, both, preferred_element_type=F32)
+                first = (2 * j).astype(F32)
+                acc = acc + jnp.where(which == first, got[:, :128], 0.0)
+                return acc + jnp.where(which == first + 1.0, got[:, 128:], 0.0)
+
+            acc = lax.fori_loop(
+                0, adapters // 2, pair, jnp.zeros((group * step, 128), F32)
+            )
+            rkrecv[c, 0, h * group * step:(h + 1) * group * step, :] = acc.astype(BF)
+            rkown[c, h * group * step:(h + 1) * group * step, :] = acc.astype(BF)
+        for k in range(1, m):
+            rank_copy(c, k).start()
+        for k in range(1, m):
+            rank_copy(c, k).wait()
+        total = rkrecv[c, 0].astype(F32)
+        for k in range(1, m):
+            total = total + rkrecv[c, k].astype(F32)
+        turned = pltpu.roll(total, 64, 1)
+        keys = jnp.where(lane < 64, total, turned)
+        vals = jnp.where(lane < 64, turned, total)
+        which = idb[c]
+        keys_by, vals_by = [], []
+        for j in range(adapters // 2):
+            mine = which == upper + float(2 * j)
+            keys_by.append(jnp.where(mine, keys, 0.0).astype(BF))
+            vals_by.append(jnp.where(mine, vals, 0.0).astype(BF))
+        keys_by = jnp.concatenate(keys_by, axis=1)
+        vals_by = jnp.concatenate(vals_by, axis=1)
+        for b in range(cols // 128):
+            mat = uv[:, b * 128:(b + 1) * 128]
+            got = jnp.dot(
+                keys_by if b % 2 == 0 else vals_by, mat, preferred_element_type=F32
+            ).astype(BF)
+            ret[c, 0, :, b * 128:(b + 1) * 128] = got[:step]
+            for k in range(1, n):
+                dout[c, k, :, b * 128:(b + 1) * 128] = got[k * step:(k + 1) * step]
+        for k in far:
+            delta_copy(c, k).start()
+        return carry
+
+    lax.fori_loop(0, CHUNKS, chunk, 0)
+
+    starts = [start_of(dp_of(k)) for k in range(n)]
+    for c in range(CHUNKS):
+        for k in range(1, n):
+            delta_copy(c, k).wait()
+
+    def finish(i, carry):
+        rs = pl.ds(pl.multiple_of(i * tile, tile), tile)
+        total = fresh[rs, :]
+        for k in range(1, m):
+            total = total + rsrecv[k, rs, :].astype(F32)
+        name = idc[rs, :]
+        away = (
+            lax.broadcasted_iota(jnp.int32, (tile, cap), 0)
+            - lax.broadcasted_iota(jnp.int32, (tile, cap), 1)
+            + i * tile
+        ).astype(F32)
+        for k in range(n):
+            low = dp_of(k) * adapters
+            mine = jnp.where((name >= low) & (name < low + adapters), 1.0, 0.0)
+            put = jnp.where(away == starts[k], mine, 0.0).astype(BF)
+            total = total + jnp.dot(
+                put, ret[:, k].reshape(cap, cols), preferred_element_type=F32
+            )
+        fresh[rs, :] = total
+        return carry
+
+    lax.fori_loop(0, rows // tile, finish, 0)
+
+
+def project(hid, ids, weight, down, up, n, m, cols, cap):
+    rows, feats = hid.shape
+    adapters = down.shape[0]
+    step = cap // CHUNKS
+    vm = pl.BlockSpec(memory_space=pltpu.VMEM)
+    hbm = pl.BlockSpec(memory_space=pl.ANY)
+    dma = pltpu.SemaphoreType.DMA
+    return pl.pallas_call(
+        functools.partial(project_kernel, n, m, adapters),
+        out_shape=jax.ShapeDtypeStruct((rows, cols), F32),
+        in_specs=[vm, vm, vm, hbm, hbm, hbm],
+        out_specs=vm,
+        scratch_shapes=[
+            pltpu.VMEM(weight.shape, BF),
+            pltpu.VMEM(down.shape, BF),
+            pltpu.VMEM((adapters * up.shape[1], cols), BF),
+            pltpu.VMEM((n, cap, feats), BF),
+            pltpu.VMEM((CHUNKS, n, step, feats), BF),
+            pltpu.VMEM((n, 16, cap), BF),
+            pltpu.VMEM((n, 16, cap), BF),
+            pltpu.VMEM((CHUNKS, n * step, 128), F32),
+            pltpu.VMEM((m, rows, cols), BF),
+            pltpu.VMEM((m, rows, cols), BF),
+            pltpu.VMEM((CHUNKS, n * step, 128), BF),
+            pltpu.VMEM((CHUNKS, m, n * step, 128), BF),
+            pltpu.VMEM((CHUNKS, n, step, cols), BF),
+            pltpu.VMEM((CHUNKS, n, step, cols), BF),
+            dma((3,)),
+            dma((CHUNKS, n)), dma((CHUNKS, n)),
+            dma((n,)), dma((n,)),
+            dma((m,)), dma((m,)),
+            dma((CHUNKS, m)), dma((CHUNKS, m)),
+            dma((CHUNKS, n)), dma((CHUNKS, n)),
+        ],
+        compiler_params=pltpu.CompilerParams(
+            collective_id=0, has_side_effects=True, vmem_limit_bytes=62 * 1024 * 1024
+        ),
+        name="project",
+    )(
+        hid, jnp.broadcast_to(ids[None, :], (8, rows)), ids[:, None], weight, down,
+        up.reshape(adapters * up.shape[1], cols),
+    )
+
+
+def attend_kernel(heads, slots, fresh, cosine, sine, bias, q, cache, new_kv, out):
+    block = fresh.shape[0]
+    span = 8
+    grp = q.shape[2]
+    dim = q.shape[3]
+    scale = 1.0 / (dim ** 0.5)
+    apart = jnp.where(
+        lax.broadcasted_iota(jnp.int32, (span * grp, span * slots), 0) // grp
+        == lax.broadcasted_iota(jnp.int32, (span * grp, span * slots), 1) // slots,
+        0.0, BIG,
+    )
+    for h in range(heads):
+        raw = fresh[:, (2 * h) * dim:(2 * h + 1) * dim]
+        key = (raw * cosine[...] + pltpu.roll(raw, dim // 2, 1) * sine[...]).astype(BF)
+        val = fresh[:, (2 * h + 1) * dim:(2 * h + 2) * dim].astype(BF)
+        new_kv[0, h] = key
+        new_kv[1, h] = val
+        key = key.astype(F32)
+        val = val.astype(F32)
+        for s in range(block // span):
+            at = slice(s * span, (s + 1) * span)
+            qs = q[h, at].reshape(span * grp, dim)
+            ks = cache[0, h, at].reshape(span * slots, dim)
+            vs = cache[1, h, at].reshape(span * slots, dim)
+            score = lax.dot_general(
+                qs, ks, (((1,), (1,)), ((), ())), preferred_element_type=F32
+            ) * scale + (apart + bias[0, s:s + 1, :])
+            near = jnp.broadcast_to(key[at][:, None, :], (span, grp, dim))
+            near = near.reshape(span * grp, dim)
+            own = jnp.sum(qs.astype(F32) * near, axis=1, keepdims=True) * scale
+            peak = jnp.maximum(jnp.max(score, axis=1, keepdims=True), own)
+            probs = jnp.exp(score - peak)
+            mine = jnp.exp(own - peak)
+            total = jnp.sum(probs, axis=1, keepdims=True) + mine
+            got = jnp.dot(probs.astype(BF), vs, preferred_element_type=F32)
+            near = jnp.broadcast_to(val[at][:, None, :], (span, grp, dim))
+            got = got + mine * near.reshape(span * grp, dim)
+            got = got * (1.0 / total)
+            out[h, at] = got.astype(BF).reshape(span, grp, dim)
+
+
+def attend_all(fresh, queries, cache, lengths):
+    heads, rows, grp, dim = queries.shape
+    slots = cache.shape[3]
+    block = 32
+    span = 8
+    inverse = rope_theta ** (-(2.0 * jnp.arange(dim // 2).astype(F32) / dim))
+    angles = lengths[:, None].astype(F32) * inverse[None, :]
+    cos, sin = jnp.cos(angles), jnp.sin(angles)
+    cosine = jnp.concatenate([cos, cos], axis=1)
+    sine = jnp.concatenate([-sin, sin], axis=1)
+    live = jnp.arange(slots)[None, :] < lengths[:, None]
+    bias = jnp.where(live, 0.0, BIG).astype(F32)
+    bias = bias.reshape(rows // block, block // span, span * slots)
+    return pl.pallas_call(
+        functools.partial(attend_kernel, heads, slots),
+        grid=(rows // block,),
+        out_shape=(
+            jax.ShapeDtypeStruct((2, heads, rows, dim), BF),
+            jax.ShapeDtypeStruct(queries.shape, BF),
+        ),
+        in_specs=[
+            pl.BlockSpec((block, fresh.shape[1]), lambda i: (i, 0)),
+            pl.BlockSpec((block, dim), lambda i: (i, 0)),
+            pl.BlockSpec((block, dim), lambda i: (i, 0)),
+            pl.BlockSpec((1, block // span, span * slots), lambda i: (i, 0, 0)),
+            pl.BlockSpec((heads, block, grp, dim), lambda i: (0, i, 0, 0)),
+            pl.BlockSpec((2, heads, block, slots, dim), lambda i: (0, 0, i, 0, 0)),
+        ],
+        out_specs=(
+            pl.BlockSpec((2, heads, block, dim), lambda i: (0, 0, i, 0)),
+            pl.BlockSpec((heads, block, grp, dim), lambda i: (0, i, 0, 0)),
+        ),
+        compiler_params=pltpu.CompilerParams(vmem_limit_bytes=48 * 1024 * 1024),
+        name="attend_all",
+    )(fresh, cosine, sine, bias, queries, cache)
+
+
+def fused_device(
+    hidden_input, key_value_weight, adapter_down_weight, adapter_up_weight, queries,
+    key_value_cache, request_adapter_index, cached_length,
+):
+    n, m = lax.axis_size("dp"), lax.axis_size("tensor")
+    rows = hidden_input.shape[0]
+    fresh = project(
+        hidden_input, request_adapter_index, key_value_weight, adapter_down_weight,
+        adapter_up_weight, n, m, adapter_up_weight.shape[2], 2 * rows // n,
+    )
+    return attend_all(fresh, queries, key_value_cache, cached_length)
 
 
 def rotate_keys(key_rows, positions):
@@ -72,13 +453,19 @@
     heads_here = queries.shape[0]
     rows_here = queries.shape[1]
     split_count = row_count // rows_here
+    if split_count == 1 and column_extent == 2 * head_dim * heads_here and head_dim == 128:
+        return fused_device(
+            hidden_input, key_value_weight, adapter_down_weight, adapter_up_weight,
+            queries, key_value_cache, request_adapter_index, cached_length,
+        )
     capacity = 2 * row_count // owner_count
     kv_heads = key_value_weight.shape[1] // (2 * head_dim)
     tensor_index = lax.axis_index("tensor")
     owner_of = request_adapter_index // adapter_total
     owner_match = (owner_of[:, None] == jnp.arange(owner_count)[None, :]).astype(jnp.int32)
     counts = jnp.sum(owner_match, axis=0)
-    starts = jnp.cumsum(counts) - counts
+    before = jnp.arange(owner_count)[None, :] < jnp.arange(owner_count)[:, None]
+    starts = jnp.sum(jnp.where(before, counts[None, :], 0), axis=1)
     slot_rows = starts[:, None] + jnp.arange(capacity)[None, :]
     padded_rows = jnp.concatenate(
         [hidden_input, jnp.zeros((capacity, feat_count), hidden_input.dtype)], axis=0

time: 643 us -> 320 us (0.50); the launches traced: 636 us -> 320 us
  waiting for transfers between devices: 339 us -> 0 us
  Pallas kernels: 0 us -> 312 us
  matrix products: 83.8 us -> 0 us
  local copies, waits for them, and re-layouts: 87.7 us -> 4.31 us
  other arithmetic: 54 us -> 2.97 us
  blocking collectives: 39.2 us -> 0 us
  starting transfers between devices: 18.1 us -> 0 us
  between operations: 14.5 us -> 0.69 us
    pallas_call x0 -> x2, Pallas kernels: none -> 312 us  [the longest x1 244 us: project(): pl.pallas_call(functools.partial(project_kernel, n, m, adapters), out_sha...]
    all_to_all x3 -> x0, waiting for transfers between devices: 211 us -> none  [the longest x1 183 us: per_device(): lax.all_to_all(send_rows, 'dp', split_axis=0, concat_axis=0, tiled=True)]
    psum x1 -> x0, waiting for transfers between devices: 128 us -> none  [per_device(): summed = lax.psum(partial_value, 'tensor')]
    dot_general x7 -> x0, matrix products: 83.8 us -> none  [the longest x1 22.9 us: attend(): jnp.einsum('igc,icd->igd', cache_weights, cache_values, preferred_element...]
    psum x1 -> x0, blocking collectives: 39.2 us -> none  [per_device(): full_rank = lax.psum(partial_rank, 'tensor').astype(jnp.bfloat16)]
    gather x4 -> x0, local copies, waits for them, and re-layouts: 35.9 us -> none  [the longest x1 19.5 us: per_device(): send_rows = jnp.take(padded_rows, slot_rows, axis=0)]
    reduce_sum x2 -> x0, other arithmetic: 30.2 us -> none  [the longest x1 30.1 us: attend(): denominator = jnp.sum(cache_exp, axis=-1) + own_exp]
    slice x2 -> x0, local copies, waits for them, and re-layouts: 24.6 us -> none  [the longest x1 24.5 us: per_device(): key_value_cache[1].reshape(flat_count, cache_slots, head_dim)]
  transfers between devices with their start and end apart: 4 -> 0, of which waited for: 3 -> 0; matrix products, arithmetic and copies ran while one was open for 15% -> 0% of each run, Pallas kernels for 0% -> 0%
where the time goes in v1:
time: 320 us
  Pallas kernels  312 us (98%)
  local copies, waits for them, and re-layouts  4.31 us (1%)
    pallas_call x1, Pallas kernels, project(): pl.pallas_call(functools.partial(project_kernel, n, m, adapters), out_sha...  244 us
    pallas_call x1, Pallas kernels, attend_all(): pl.pallas_call(functools.partial(attend_kernel, heads, slots), grid=(rows...  68.6 us

profile of v1, /device:TPU:1, one launch (start us, length us, event | category | flops | bytes accessed | tf_op | source)
XLA Modules:
  0.0 320.1 jit_solution(9705317091382597193)
XLA Ops:
  0.6 0.7 convert_element_type.11
  1.3 0.1 lt.23
  1.4 1.3 broadcast_in_dim.10.idr
  2.7 0.8 lt.25
  3.5 0.2 lt.26
  3.7 0.2 lt.27
  4.0 1.7 copy.10.idc
  5.7 243.5 %project.1.fresh = f32[1024,512]{1,0:T(8,128)} custom-call(bf16[1024,2048]{1,0:T(8,128)(2,1)} %hid.1, s32[8,1024]{1,0:T(8,128)} %broadcast_in_dim.10.idr, s32[1024,1]{1,0:T(8,128)} %copy.10.idc, bf16[2048,2048]{1,0:T(8,128)(2,1)} %w_hbm.1, bf16[16,2048,128]{2,1,0:T(8,128)(2,1)} %dn_hbm.1, bf16[1024,512]{1,0:T(8,128)(2,1)} %bitcast.4), custom_call_target="tpu_custom_call" | custom-call | tf_op jit(solution)/shard_map/project/pallas_call | solution.py:262
  249.2 0.0 copy-start
  249.2 1.9 fusion
  251.1 0.3 pad_maximum_fusion
  251.5 0.0 copy-done
  251.5 68.6 %attend_all.1 = (bf16[2,2,1024,128]{3,2,1,0:T(8,128)(2,1)}, bf16[2,1024,8,128]{3,2,1,0:T(8,128)(2,1)}) custom-call(f32[1024,512]{1,0:T(8,128)S(1)} %copy-done, f32[1024,128]{1,0:T(8,128)S(1)} %get-tuple-element.5.cosine, f32[1024,128]{1,0:T(8,128)S(1)} %get-tuple-element.6.sine, f32[32,4,256]{2,1,0:T(4,128)S(1)} %compare_select_fusion.bias, ...), custom_call_target="tpu_custom_call" | custom-call | tf_op jit(solution)/shard_map/attend_all/pallas_call | solution.py:353
  (3 shorter events, 0.0 us)
Async XLA Ops:
  249.2 2.3 copy-start

commit v2 on v1

--- a/solution.py
+++ b/solution.py
@@ -315,32 +315,52 @@
         new_kv[1, h] = val
         key = key.astype(F32)
         val = val.astype(F32)
-        for s in range(block // span):
-            at = slice(s * span, (s + 1) * span)
-            qs = q[h, at].reshape(span * grp, dim)
-            ks = cache[0, h, at].reshape(span * slots, dim)
-            vs = cache[1, h, at].reshape(span * slots, dim)
-            score = lax.dot_general(
-                qs, ks, (((1,), (1,)), ((), ())), preferred_element_type=F32
-            ) * scale + (apart + bias[0, s:s + 1, :])
-            near = jnp.broadcast_to(key[at][:, None, :], (span, grp, dim))
-            near = near.reshape(span * grp, dim)
-            own = jnp.sum(qs.astype(F32) * near, axis=1, keepdims=True) * scale
-            peak = jnp.maximum(jnp.max(score, axis=1, keepdims=True), own)
-            probs = jnp.exp(score - peak)
-            mine = jnp.exp(own - peak)
-            total = jnp.sum(probs, axis=1, keepdims=True) + mine
-            got = jnp.dot(probs.astype(BF), vs, preferred_element_type=F32)
-            near = jnp.broadcast_to(val[at][:, None, :], (span, grp, dim))
-            got = got + mine * near.reshape(span * grp, dim)
-            got = got * (1.0 / total)
-            out[h, at] = got.astype(BF).reshape(span, grp, dim)
+        for first in range(0, block // span, 4):
+            spans = [slice((first + s) * span, (first + s + 1) * span) for s in range(4)]
+            qs = [q[h, at].reshape(span * grp, dim) for at in spans]
+            scores = [
+                lax.dot_general(
+                    qs[s], cache[0, h, spans[s]].reshape(span * slots, dim),
+                    (((1,), (1,)), ((), ())), preferred_element_type=F32,
+                )
+                for s in range(4)
+            ]
+            near = [
+                jnp.broadcast_to(key[at][:, None, :], (span, grp, dim)).reshape(span * grp, dim)
+                for at in spans
+            ]
+            own = [
+                jnp.sum(qs[s].astype(F32) * near[s], axis=1, keepdims=True) * scale
+                for s in range(4)
+            ]
+            scores = [
+                scores[s] * scale + (apart + bias[0, first + s:first + s + 1, :])
+                for s in range(4)
+            ]
+            peaks = [
+                jnp.maximum(jnp.max(scores[s], axis=1, keepdims=True), own[s]) for s in range(4)
+            ]
+            probs = [jnp.exp(scores[s] - peaks[s]) for s in range(4)]
+            mine = [jnp.exp(own[s] - peaks[s]) for s in range(4)]
+            totals = [jnp.sum(probs[s], axis=1, keepdims=True) + mine[s] for s in range(4)]
+            got = [
+                jnp.dot(
+                    probs[s].astype(BF), cache[1, h, spans[s]].reshape(span * slots, dim),
+                    preferred_element_type=F32,
+                )
+                for s in range(4)
+            ]
+            for s in range(4):
+                near = jnp.broadcast_to(val[spans[s]][:, None, :], (span, grp, dim))
+                full = got[s] + mine[s] * near.reshape(span * grp, dim)
+                full = full * (1.0 / totals[s])
+                out[h, spans[s]] = full.astype(BF).reshape(span, grp, dim)
 
 
 def attend_all(fresh, queries, cache, lengths):
     heads, rows, grp, dim = queries.shape
     slots = cache.shape[3]
-    block = 32
+    block = 64
     span = 8
     inverse = rope_theta ** (-(2.0 * jnp.arange(dim // 2).astype(F32) / dim))
     angles = lengths[:, None].astype(F32) * inverse[None, :]

time: 320 us -> 280 us (0.88)
  Pallas kernels: 312 us -> 271 us
    pallas_call x1, Pallas kernels: 68.6 us -> 27.5 us  [attend_all(): pl.pallas_call(functools.partial(attend_kernel, heads, slots), grid=(rows...]
where the time goes in v2:
time: 280 us; the launch traced here: 279 us
  Pallas kernels  271 us (97%)
  local copies, waits for them, and re-layouts  4.24 us (2%)
  other arithmetic  2.95 us (1%)
    pallas_call x1, Pallas kernels, project(): pl.pallas_call(functools.partial(project_kernel, n, m, adapters), out_sha...  244 us
    pallas_call x1, Pallas kernels, attend_all(): pl.pallas_call(functools.partial(attend_kernel, heads, slots), grid=(rows...  27.5 us

profile of v2, /device:TPU:1, one launch (start us, length us, event | category | flops | bytes accessed | tf_op | source)
XLA Modules:
  0.0 278.9 jit_solution(16530322636303110554)
XLA Ops:
  0.6 0.7 convert_element_type.11
  1.3 0.1 lt.23
  1.4 1.3 broadcast_in_dim.10.idr
  2.7 0.8 lt.25
  3.5 0.2 lt.26
  3.7 0.2 lt.27
  3.9 1.7 copy.10.idc
  5.6 243.5 %project.1.fresh = f32[1024,512]{1,0:T(8,128)} custom-call(bf16[1024,2048]{1,0:T(8,128)(2,1)} %hid.1, s32[8,1024]{1,0:T(8,128)} %broadcast_in_dim.10.idr, s32[1024,1]{1,0:T(8,128)} %copy.10.idc, bf16[2048,2048]{1,0:T(8,128)(2,1)} %w_hbm.1, bf16[16,2048,128]{2,1,0:T(8,128)(2,1)} %dn_hbm.1, bf16[1024,512]{1,0:T(8,128)(2,1)} %bitcast.4), custom_call_target="tpu_custom_call" | custom-call | tf_op jit(solution)/shard_map/project/pallas_call | solution.py:262
  249.1 0.0 copy-start
  249.2 1.9 fusion
  251.1 0.3 pad_maximum_fusion
  251.4 0.0 copy-done
  251.4 27.5 %attend_all.1 = (bf16[2,2,1024,128]{3,2,1,0:T(8,128)(2,1)}, bf16[2,1024,8,128]{3,2,1,0:T(8,128)(2,1)}) custom-call(f32[1024,512]{1,0:T(8,128)S(1)} %copy-done, f32[1024,128]{1,0:T(8,128)S(1)} %get-tuple-element.5.cosine, f32[1024,128]{1,0:T(8,128)S(1)} %get-tuple-element.6.sine, f32[16,8,256]{2,1,0:T(8,128)S(1)} %compare_select_fusion.bias, ...), custom_call_target="tpu_custom_call" | custom-call | tf_op jit(solution)/shard_map/attend_all/pallas_call | solution.py:373
  (3 shorter events, 0.0 us)
Async XLA Ops:
  249.1 2.3 copy-start
